TPU v7x, 32 devices: a whole 2x2x4 slice. The times are simulated.
32 devices in a mesh: dp: 4 (over y, x), seq: 8 (over z, core).
Axes of the slice: x: 2, y: 2, z: 4, core: 2. Of those that a mesh axis runs over, the one named last changes fastest.
Arguments:
- tokens: bfloat16 [4, 1024, 5120], P('dp', 'seq'), may hold values from -6 to 6
- base_query: bfloat16 [4, 1024, 2560], P('dp', 'seq'), may hold values from -96 to 96
- k_base: bfloat16 [4, 1024, 2560], P('dp', 'seq'), may hold values from -4 to 4
- v_base: bfloat16 [4, 1024, 2560], P('dp', 'seq'), may hold values from -6 to 6
- cotangent: bfloat16 [4, 1024, 2560], P('dp', 'seq'), may hold values from -0.018676758 to 0.018676758
- adapter_down: bfloat16 [5120, 256], replicated, may hold values from -0.078125 to 0.078125
- adapter_up_weight: bfloat16 [256, 2560], replicated, may hold values from -1 to 1
- gate_weight: bfloat16 [8, 5120], replicated, may hold values from -0.078125 to 0.078125
Outputs:
- attended: bfloat16 [4, 1024, 2560], P('dp', 'seq')
- gate_grad: float32 [8, 5120], replicated
All inputs are finite; a program needn't handle non-finite values.
Results may differ from a plain program's by a relative error of at most 0.03.
Values may be sent and summed in bfloat16 or wider, within the bound.
A program may use at most 192 MiB of HBM per device.

v0:
```python
import functools

import jax
import jax.numpy as jnp
from jax import lax
from jax.experimental import pallas as pl
from jax.experimental.pallas import tpu as pltpu
from jax.sharding import PartitionSpec as P

HEAD_DIM = 128
ADAPTER_SCALE = 2.0
MASKED = -1e30
MESH = pl.DeviceIdType.MESH
F32 = jnp.float32
BF16 = jnp.bfloat16
NT = (((1,), (1,)), ((), ()))
NN = (((1,), (0,)), ((), ()))


def dot(a, b, dims=NN, precision=None):
    return lax.dot_general(a, b, dims, preferred_element_type=F32, precision=precision)


def kernel(
    chips, chunks, heads, n_dp,
    k_hbm, v_hbm, bq_hbm, cot_hbm, tok_hbm, down_hbm, up_hbm, gw_hbm,
    out_ref, gg_ref,
    kv, bq, cot, tok, down, up, gw, low, mixed, dmix, gates_ref, part, ra, rb, rc, mine,
    own_sem, load_sem, up_send, up_recv, mate_send, mate_recv,
    a_send, a_recv, b_send, b_recv, c_send, c_recv,
):
    n_seq = 2 * chips
    me = lax.axis_index("seq")
    dp = lax.axis_index("dp")
    z = me // 2
    core = lax.rem(me, 2)
    mate = me + 1 - 2 * core
    rows = tok.shape[0]
    wide = heads * HEAD_DIM
    scale = HEAD_DIM ** (-0.5)

    barrier = pltpu.get_barrier_semaphore()
    for d in range(1, n_seq):
        pl.semaphore_signal(
            barrier, inc=1, device_id={"seq": lax.rem(me + d, n_seq)}, device_id_type=MESH
        )
    for d in range(1, n_dp):
        pl.semaphore_signal(
            barrier, inc=1, device_id={"dp": lax.rem(dp + d, n_dp)}, device_id_type=MESH
        )

    def own_copies(c):
        cols = pl.ds(c * wide, wide)
        return [
            pltpu.make_async_copy(src.at[0, :, cols], kv.at[c, z, core, i], own_sem.at[c, i])
            for i, src in enumerate((k_hbm, v_hbm))
        ]

    for c in range(chunks):
        for copy in own_copies(c):
            copy.start()
    loads = [
        pltpu.make_async_copy(src, dst, load_sem.at[i])
        for i, (src, dst) in enumerate(
            (
                (tok_hbm.at[0], tok), (gw_hbm, gw), (down_hbm, down), (up_hbm, up),
                (bq_hbm.at[0], bq), (cot_hbm.at[0], cot),
            )
        )
    ]
    for copy in loads:
        copy.start()
    pl.semaphore_wait(barrier, n_seq - 1 + n_dp - 1)

    def to_next(c, j):
        block = kv.at[c, j, core]
        return pltpu.make_async_remote_copy(
            src_ref=block, dst_ref=block, send_sem=up_send.at[c, j], recv_sem=up_recv.at[c, j],
            device_id={"seq": lax.rem(me + 2, n_seq)}, device_id_type=MESH,
        )

    def to_mate(c, j):
        block = kv.at[c, j, core]
        return pltpu.make_async_remote_copy(
            src_ref=block, dst_ref=block, send_sem=mate_send.at[c, j], recv_sem=mate_recv.at[c, j],
            device_id={"seq": mate}, device_id_type=MESH,
        )

    def from_mate(c, j):
        block = kv.at[c, j, 1 - core]
        return pltpu.make_async_remote_copy(
            src_ref=block, dst_ref=block, send_sem=mate_send.at[c, j], recv_sem=mate_recv.at[c, j],
            device_id={"seq": mate}, device_id_type=MESH,
        )

    for c in range(chunks):
        for copy in own_copies(c):
            copy.wait()

        @pl.when(z < chips - 1)
        def _():
            to_next(c, z).start()

        to_mate(c, z).start()

    loads[0].wait()
    loads[1].wait()
    logits = dot(tok[...], gw[...], NT)
    logits = jnp.exp(logits - jnp.max(logits, axis=-1, keepdims=True))
    gates = logits / jnp.sum(logits, axis=-1, keepdims=True)
    gates_ref[...] = gates
    experts = gates.shape[1]
    total_rank = low.shape[1]
    rank = total_rank // experts
    spread = (
        lax.broadcasted_iota(jnp.int32, (experts, total_rank), 1) // rank
        == lax.broadcasted_iota(jnp.int32, (experts, total_rank), 0)
    ).astype(F32)
    loads[2].wait()
    low_b = dot(tok[...], down[...]).astype(BF16)
    low[...] = low_b
    wide_gates = dot(gates, spread, precision=lax.Precision.HIGHEST)
    mixed[...] = (low_b.astype(F32) * wide_gates).astype(BF16)
    dmix[...] = jnp.zeros_like(dmix)
    for copy in loads[3:]:
        copy.wait()

    def chunk_step(c, carry):
        for back in range(1, chips):
            j = z - back

            @pl.when(j >= 0)
            def _():
                to_next(c, j).wait_recv()

                @pl.when(z < chips - 1)
                def _():
                    to_next(c, j).start()

                to_mate(c, j).start()

        for back in range(chips):
            j = z - back

            @pl.when(j >= 0)
            def _():
                from_mate(c, j).wait_recv()

        cols = pl.ds(pl.multiple_of(c * wide, wide), wide)
        up_c = up[:, cols]
        query = (
            bq[:, cols].astype(F32) + ADAPTER_SCALE * dot(mixed[...], up_c)
        ).astype(BF16)
        cot_c = cot[:, cols]
        outs = []
        grads = []
        q_pos = core * rows + lax.broadcasted_iota(jnp.int32, (rows, 2 * rows), 0)
        visible = lax.broadcasted_iota(jnp.int32, (rows, 2 * rows), 1) <= q_pos
        qs = [query[:, h * HEAD_DIM : (h + 1) * HEAD_DIM] for h in range(heads)]
        cs = [cot_c[:, h * HEAD_DIM : (h + 1) * HEAD_DIM] for h in range(heads)]

        def block(j, states, masked):
            new_states = []
            for h in range(heads):
                hcols = slice(h * HEAD_DIM, (h + 1) * HEAD_DIM)
                keys = kv[c, j, :, 0, :, hcols].reshape(2 * rows, HEAD_DIM)
                values = kv[c, j, :, 1, :, hcols].reshape(2 * rows, HEAD_DIM)
                scores = dot(qs[h], keys, NT) * scale
                slopes = dot(cs[h], values, NT)
                if masked:
                    scores = jnp.where(visible, scores, MASKED)
                top = jnp.max(scores, axis=-1, keepdims=True)
                if states is not None:
                    old_top, old_sum, old_delta, old_vk, old_grad = states[h]
                    top = jnp.maximum(old_top, top)
                weights = jnp.exp(scores - top)
                products = weights * slopes
                total = jnp.sum(weights, axis=-1, keepdims=True)
                delta = jnp.sum(products, axis=-1, keepdims=True)
                vk = dot(weights.astype(BF16), jnp.concatenate([values, keys], axis=1))
                grad = dot(products.astype(BF16), keys)
                if states is not None:
                    fade = jnp.exp(old_top - top)
                    total = total + old_sum * fade
                    delta = delta + old_delta * fade
                    vk = vk + old_vk * fade
                    grad = grad + old_grad * fade
                new_states.append((top, total, delta, vk, grad))
            return tuple(new_states)

        states = block(z, None, True)
        states = lax.fori_loop(0, z, lambda j, st: block(j, st, False), states)
        for top, total, delta, vk, grad in states:
            inverse = 1.0 / total
            outs.append((vk[:, :HEAD_DIM] * inverse).astype(BF16))
            grads.append(
                (
                    scale
                    * (
                        grad * inverse
                        - (delta * inverse) * (vk[:, HEAD_DIM:] * inverse)
                    )
                ).astype(BF16)
            )
        out_ref[0, :, cols] = jnp.concatenate(outs, axis=1)
        dmix[...] += dot(jnp.concatenate(grads, axis=1), up_c, NT)
        return carry

    lax.fori_loop(0, chunks, chunk_step, 0)

    dgates = dot(
        ADAPTER_SCALE * dmix[...] * low[...].astype(F32), spread, NT,
        precision=lax.Precision.HIGHEST,
    )
    gates = gates_ref[...]
    dlogits = gates * (dgates - jnp.sum(gates * dgates, axis=-1, keepdims=True))
    partial = dot(dlogits.astype(BF16), tok[...], (((0,), (0,)), ((), ())))

    piece = part.shape[2]
    full = partial.shape[1]
    for n in range(n_seq):
        have = min(max(full - n * piece, 0), piece)
        if have:
            part[n, :, :have] = partial[:, n * piece : n * piece + have]
        if have < piece:
            part[n, :, have:] = jnp.zeros((part.shape[1], piece - have), F32)

    def exchange(axis, index, count, source, target, send, recv):
        copies = []
        for d in range(1, count):
            peer = lax.rem(index + d, count)
            copies.append(
                pltpu.make_async_remote_copy(
                    src_ref=source(peer), dst_ref=target.at[index],
                    send_sem=send.at[d], recv_sem=recv.at[index],
                    device_id={axis: peer}, device_id_type=MESH,
                )
            )
        for copy in copies:
            copy.start()
        for d in range(1, count):
            peer = lax.rem(index + d, count)
            pltpu.make_async_remote_copy(
                src_ref=source(peer), dst_ref=target.at[peer],
                send_sem=send.at[d], recv_sem=recv.at[peer],
                device_id={axis: peer}, device_id_type=MESH,
            ).wait_recv()
        return copies

    ra[me] = part[me]
    sent = exchange("seq", me, n_seq, lambda peer: part.at[peer], ra, a_send, a_recv)
    total = ra[0]
    for n in range(1, n_seq):
        total = total + ra[n]
    rb[dp] = total
    sent += exchange("dp", dp, n_dp, lambda peer: rb.at[dp], rb, b_send, b_recv)
    total = rb[0]
    for n in range(1, n_dp):
        total = total + rb[n]
    rc[me] = total
    sent += exchange("seq", me, n_seq, lambda peer: rc.at[me], rc, c_send, c_recv)
    for n in range(n_seq):
        have = min(max(full - n * piece, 0), piece)
        if have:
            gg_ref[:, n * piece : n * piece + have] = rc[n, :, :have]
    for copy in sent:
        copy.wait_send()

    def drain(c, carry):
        for back in range(chips):
            j = z - back

            @pl.when(j >= 0)
            def _():
                @pl.when(z < chips - 1)
                def _():
                    to_next(c, j).wait_send()

                to_mate(c, j).wait_send()

        return carry

    lax.fori_loop(0, chunks, drain, 0)


def shards(n_dp, n_seq, *args):
    tokens, base_query, k_base, v_base, cotangent, down, up, gate_weight = args
    rows, width = tokens.shape[1], base_query.shape[2]
    model, experts, total_rank = tokens.shape[2], gate_weight.shape[0], down.shape[1]
    head_count = width // HEAD_DIM
    heads = max(h for h in range(1, 5) if head_count % h == 0)
    chunks, chips = head_count // heads, n_seq // 2
    wide = heads * HEAD_DIM
    piece = -(-(model // 128) // n_seq) * 128
    any_spec = pl.BlockSpec(memory_space=pl.ANY)
    vmem_spec = pl.BlockSpec(memory_space=pltpu.VMEM)
    dma = pltpu.SemaphoreType.DMA
    return pl.pallas_call(
        functools.partial(kernel, chips, chunks, heads, n_dp),
        out_shape=(
            jax.ShapeDtypeStruct((1, rows, width), BF16),
            jax.ShapeDtypeStruct((experts, model), F32),
        ),
        in_specs=[any_spec] * 8,
        out_specs=(vmem_spec, vmem_spec),
        scratch_shapes=[
            pltpu.VMEM((chunks, chips, 2, 2, rows, wide), BF16),
            pltpu.VMEM((rows, width), BF16),
            pltpu.VMEM((rows, width), BF16),
            pltpu.VMEM((rows, model), BF16),
            pltpu.VMEM((model, total_rank), BF16),
            pltpu.VMEM((total_rank, width), BF16),
            pltpu.VMEM((experts, model), BF16),
            pltpu.VMEM((rows, total_rank), BF16),
            pltpu.VMEM((rows, total_rank), BF16),
            pltpu.VMEM((rows, total_rank), F32),
            pltpu.VMEM((rows, experts), F32),
            pltpu.VMEM((n_seq, experts, piece), F32),
            pltpu.VMEM((n_seq, experts, piece), F32),
            pltpu.VMEM((n_dp, experts, piece), F32),
            pltpu.VMEM((n_seq, experts, piece), F32),
            pltpu.VMEM((experts, piece), F32),
            dma((chunks, 2)),
            dma((6,)),
            dma((chunks, chips)),
            dma((chunks, chips)),
            dma((chunks, chips)),
            dma((chunks, chips)),
            dma((n_seq,)),
            dma((n_seq,)),
            dma((n_dp,)),
            dma((n_dp,)),
            dma((n_seq,)),
            dma((n_seq,)),
        ],
        compiler_params=pltpu.CompilerParams(
            collective_id=0, has_side_effects=True, vmem_limit_bytes=56 * 1024 * 1024
        ),
        cost_estimate=pl.CostEstimate(
            flops=10 * rows * rows * n_seq * width, bytes_accessed=16 * rows * width,
            transcendentals=rows * rows * n_seq * head_count,
        ),
    )(k_base, v_base, base_query, cotangent, tokens, down, up, gate_weight)


def solution(mesh):
    split = P("dp", "seq", None)
    return jax.shard_map(
        functools.partial(shards, mesh.shape["dp"], mesh.shape["seq"]),
        mesh=mesh,
        in_specs=(split, split, split, split, split, P(), P(), P()),
        out_specs=(split, P()),
        check_vma=False,
    )
```

profile of v0, /device:TPU:0, one launch (start us, length us, event | category | flops | bytes accessed | tf_op | source)
XLA Modules:
  0.0 120.9 jit_solution(11264394668363902015)
XLA Ops:
  0.6 117.5 %shard_map.95 = (bf16[1,128,2560]{2,1,0:T(8,128)(2,1)}, f32[8,5120]{1,0:T(8,128)}) custom-call(bf16[1,128,2560]{2,1,0:T(8,128)(2,1)} %k_hbm.1, bf16[1,128,2560]{2,1,0:T(8,128)(2,1)} %v_hbm.1, bf16[1,128,2560]{2,1,0:T(8,128)(2,1)} %bq_hbm.1, bf16[1,128,2560]{2,1,0:T(8,128)(2,1)} %cot_hbm.1, bf16[1,128,5120]{2,1,0:T(8,128)(2,1)} %tok_hbm.1, ...), custom_call_target="tpu_custom_call" | custom-call | flops 3355443200 | bytes 5242880 | tf_op jit(solution)/shard_map/pallas_call | solution.py:298
  118.2 0.0 copy-start
  118.2 2.0 %copy.12 = bf16[1,128,2560]{2,1,0:T(8,128)(2,1)} copy(bf16[1,128,2560]{2,1,0:T(8,128)(2,1)} %get-tuple-element.4) | data formatting | bytes 1310720
  120.2 0.0 copy-done
  120.2 0.7 copy.13
Async XLA Ops:
  118.2 2.0 %copy-start = (f32[8,5120]{1,0:T(8,128)S(1)}, f32[8,5120]{1,0:T(8,128)}, u32[]{:S(2)}) copy-start(f32[8,5120]{1,0:T(8,128)} %get-tuple-element.5) | copy-start | bytes 491524
where the time goes:
time: 121 us
  Pallas kernels  118 us (98%)
  local copies, waits for them, and re-layouts  2.67 us (2%)
    pallas_call x1, Pallas kernels, shards(): pl.pallas_call(functools.partial(kernel, chips, chunks, heads, n_dp), out...  118 us
    unnamed x4, local copies, waits for them, and re-layouts  2.67 us

commit v1 on v0

--- a/solution.py
+++ b/solution.py
@@ -25,8 +25,9 @@
     chips, chunks, heads, n_dp,
     k_hbm, v_hbm, bq_hbm, cot_hbm, tok_hbm, down_hbm, up_hbm, gw_hbm,
     out_ref, gg_ref,
-    kv, bq, cot, tok, down, up, gw, low, mixed, dmix, gates_ref, part, ra, rb, rc, mine,
+    kv, qb, ob, back, bq, tok, down, up, gw, low, dmix, gates_ref, part, ra, rb, rc,
     own_sem, load_sem, up_send, up_recv, mate_send, mate_recv,
+    q_send, q_recv, ret_send, ret_recv,
     a_send, a_recv, b_send, b_recv, c_send, c_recv,
 ):
     n_seq = 2 * chips
@@ -49,6 +50,9 @@
             barrier, inc=1, device_id={"dp": lax.rem(dp + d, n_dp)}, device_id_type=MESH
         )
 
+    def depth_of(c):
+        return min(max(0, 2 - (c + 1) // 2), chips - 1)
+
     def own_copies(c):
         cols = pl.ds(c * wide, wide)
         return [
@@ -64,44 +68,70 @@
         for i, (src, dst) in enumerate(
             (
                 (tok_hbm.at[0], tok), (gw_hbm, gw), (down_hbm, down), (up_hbm, up),
-                (bq_hbm.at[0], bq), (cot_hbm.at[0], cot),
+                (bq_hbm.at[0], bq),
             )
         )
+    ] + [
+        pltpu.make_async_copy(
+            cot_hbm.at[0, :, pl.ds(c * wide, wide)], qb.at[c, 0, 1], load_sem.at[5 + c]
+        )
+        for c in range(chunks)
     ]
     for copy in loads:
         copy.start()
     pl.semaphore_wait(barrier, n_seq - 1 + n_dp - 1)
 
+    def block_copy(c, j, side, send, recv, target):
+        block = kv.at[c, j, side]
+        return pltpu.make_async_remote_copy(
+            src_ref=block, dst_ref=block, send_sem=send.at[c, j], recv_sem=recv.at[c, j],
+            device_id={"seq": target}, device_id_type=MESH,
+        )
+
     def to_next(c, j):
-        block = kv.at[c, j, core]
+        return block_copy(c, j, core, up_send, up_recv, lax.rem(me + 2, n_seq))
+
+    def to_mate(c, j):
+        return block_copy(c, j, core, mate_send, mate_recv, mate)
+
+    def from_mate(c, j):
+        return block_copy(c, j, 1 - core, mate_send, mate_recv, mate)
+
+    def host_of(c):
+        return 2 * (chips - 1 - depth_of(c)) + core
+
+    def to_host(c):
+        return block_copy(c, z, core, up_send, up_recv, host_of(c))
+
+    def query_to_host(c, d):
         return pltpu.make_async_remote_copy(
-            src_ref=block, dst_ref=block, send_sem=up_send.at[c, j], recv_sem=up_recv.at[c, j],
-            device_id={"seq": lax.rem(me + 2, n_seq)}, device_id_type=MESH,
-        )
-
-    def to_mate(c, j):
-        block = kv.at[c, j, core]
+            src_ref=qb.at[c, 0], dst_ref=qb.at[c, d], send_sem=q_send.at[c],
+            recv_sem=q_recv.at[c, d], device_id={"seq": host_of(c)}, device_id_type=MESH,
+        )
+
+    def give_back(c, d):
         return pltpu.make_async_remote_copy(
-            src_ref=block, dst_ref=block, send_sem=mate_send.at[c, j], recv_sem=mate_recv.at[c, j],
-            device_id={"seq": mate}, device_id_type=MESH,
-        )
-
-    def from_mate(c, j):
-        block = kv.at[c, j, 1 - core]
-        return pltpu.make_async_remote_copy(
-            src_ref=block, dst_ref=block, send_sem=mate_send.at[c, j], recv_sem=mate_recv.at[c, j],
-            device_id={"seq": mate}, device_id_type=MESH,
-        )
-
-    for c in range(chunks):
+            src_ref=ob.at[c, d], dst_ref=back.at[c], send_sem=ret_send.at[c, d],
+            recv_sem=ret_recv.at[c], device_id={"seq": lax.rem(me + 2 * d, n_seq)},
+            device_id_type=MESH,
+        )
+
+    for c in range(chunks):
+        host = chips - 1 - depth_of(c)
         for copy in own_copies(c):
             copy.wait()
 
-        @pl.when(z < chips - 1)
+        @pl.when(z < host)
         def _():
             to_next(c, z).start()
 
-        to_mate(c, z).start()
+        @pl.when(z <= host)
+        def _():
+            to_mate(c, z).start()
+
+        @pl.when(z > host)
+        def _():
+            to_host(c).start()
 
     loads[0].wait()
     loads[1].wait()
@@ -120,53 +150,35 @@
     low_b = dot(tok[...], down[...]).astype(BF16)
     low[...] = low_b
     wide_gates = dot(gates, spread, precision=lax.Precision.HIGHEST)
-    mixed[...] = (low_b.astype(F32) * wide_gates).astype(BF16)
+    mixed = (low_b.astype(F32) * wide_gates).astype(BF16)
     dmix[...] = jnp.zeros_like(dmix)
     for copy in loads[3:]:
         copy.wait()
-
-    def chunk_step(c, carry):
-        for back in range(1, chips):
-            j = z - back
-
-            @pl.when(j >= 0)
-            def _():
-                to_next(c, j).wait_recv()
-
-                @pl.when(z < chips - 1)
-                def _():
-                    to_next(c, j).start()
-
-                to_mate(c, j).start()
-
-        for back in range(chips):
-            j = z - back
-
-            @pl.when(j >= 0)
-            def _():
-                from_mate(c, j).wait_recv()
-
-        cols = pl.ds(pl.multiple_of(c * wide, wide), wide)
-        up_c = up[:, cols]
-        query = (
-            bq[:, cols].astype(F32) + ADAPTER_SCALE * dot(mixed[...], up_c)
+    for c in range(chunks):
+        cols = slice(c * wide, (c + 1) * wide)
+        qb[c, 0, 0] = (
+            bq[:, cols].astype(F32) + ADAPTER_SCALE * dot(mixed, up[:, cols])
         ).astype(BF16)
-        cot_c = cot[:, cols]
-        outs = []
-        grads = []
+        for d in range(1, depth_of(c) + 1):
+
+            @pl.when(z == chips - 1 - depth_of(c) + d)
+            def _():
+                query_to_host(c, d).start()
+
+    def attend(c, d):
+        cols = slice(c * wide, (c + 1) * wide)
         q_pos = core * rows + lax.broadcasted_iota(jnp.int32, (rows, 2 * rows), 0)
         visible = lax.broadcasted_iota(jnp.int32, (rows, 2 * rows), 1) <= q_pos
-        qs = [query[:, h * HEAD_DIM : (h + 1) * HEAD_DIM] for h in range(heads)]
-        cs = [cot_c[:, h * HEAD_DIM : (h + 1) * HEAD_DIM] for h in range(heads)]
+        heads_at = [slice(h * HEAD_DIM, (h + 1) * HEAD_DIM) for h in range(heads)]
 
         def block(j, states, masked):
             new_states = []
             for h in range(heads):
-                hcols = slice(h * HEAD_DIM, (h + 1) * HEAD_DIM)
+                hcols = heads_at[h]
                 keys = kv[c, j, :, 0, :, hcols].reshape(2 * rows, HEAD_DIM)
                 values = kv[c, j, :, 1, :, hcols].reshape(2 * rows, HEAD_DIM)
-                scores = dot(qs[h], keys, NT) * scale
-                slopes = dot(cs[h], values, NT)
+                scores = dot(qb[c, d, 0, :, hcols], keys, NT) * scale
+                slopes = dot(qb[c, d, 1, :, hcols], values, NT)
                 if masked:
                     scores = jnp.where(visible, scores, MASKED)
                 top = jnp.max(scores, axis=-1, keepdims=True)
@@ -188,8 +200,10 @@
                 new_states.append((top, total, delta, vk, grad))
             return tuple(new_states)
 
-        states = block(z, None, True)
-        states = lax.fori_loop(0, z, lambda j, st: block(j, st, False), states)
+        states = block(z + d, None, True)
+        states = lax.fori_loop(0, z + d, lambda j, st: block(j, st, False), states)
+        outs = []
+        grads = []
         for top, total, delta, vk, grad in states:
             inverse = 1.0 / total
             outs.append((vk[:, :HEAD_DIM] * inverse).astype(BF16))
@@ -202,11 +216,72 @@
                     )
                 ).astype(BF16)
             )
-        out_ref[0, :, cols] = jnp.concatenate(outs, axis=1)
-        dmix[...] += dot(jnp.concatenate(grads, axis=1), up_c, NT)
-        return carry
-
-    lax.fori_loop(0, chunks, chunk_step, 0)
+        return (
+            jnp.concatenate(outs, axis=1),
+            dot(jnp.concatenate(grads, axis=1), up[:, cols], NT),
+        )
+
+    def own_step(c):
+        host = chips - 1 - depth_of(c)
+        for gap in range(1, host + 1):
+
+            @pl.when((z >= gap) & (z <= host))
+            def _():
+                to_next(c, z - gap).wait_recv()
+
+                @pl.when(z < host)
+                def _():
+                    to_next(c, z - gap).start()
+
+                to_mate(c, z - gap).start()
+
+        @pl.when(z <= host)
+        def _():
+            def arrive(gap, carry):
+                from_mate(c, z - gap).wait_recv()
+                return carry
+
+            lax.fori_loop(0, z + 1, arrive, 0)
+            attended, term = attend(c, 0)
+            out_ref[0, :, c * wide : (c + 1) * wide] = attended
+            dmix[...] += term
+
+    def hosted_step(c):
+        host = chips - 1 - depth_of(c)
+
+        @pl.when(z == host)
+        def _():
+            for d in range(1, depth_of(c) + 1):
+                to_next(c, z + d).wait_recv()
+                to_mate(c, z + d).start()
+            for d in range(1, depth_of(c) + 1):
+                from_mate(c, z + d).wait_recv()
+                query_to_host(c, d).wait_recv()
+                attended, term = attend(c, d)
+                ob[c, d, :, :wide] = attended
+                ob[c, d, :, wide:] = term.astype(BF16)
+                give_back(c, d).start()
+
+    deep = [c for c in range(chunks) if depth_of(c) > 1]
+    waiting = []
+    for c in range(chunks):
+        own_step(c)
+        if c == chunks - 1:
+            waiting += deep
+        for late in waiting:
+            hosted_step(late)
+        waiting = [c] if depth_of(c) == 1 else []
+    for late in waiting:
+        hosted_step(late)
+
+    for c in range(chunks):
+        if depth_of(c):
+
+            @pl.when(z > chips - 1 - depth_of(c))
+            def _():
+                give_back(c, 1).wait_recv()
+                out_ref[0, :, c * wide : (c + 1) * wide] = back[c, :, :wide]
+                dmix[...] += back[c, :, wide:].astype(F32)
 
     dgates = dot(
         ADAPTER_SCALE * dmix[...] * low[...].astype(F32), spread, NT,
@@ -266,21 +341,34 @@
     for copy in sent:
         copy.wait_send()
 
-    def drain(c, carry):
-        for back in range(chips):
-            j = z - back
-
-            @pl.when(j >= 0)
-            def _():
-                @pl.when(z < chips - 1)
-                def _():
-                    to_next(c, j).wait_send()
-
-                to_mate(c, j).wait_send()
-
-        return carry
-
-    lax.fori_loop(0, chunks, drain, 0)
+    for c in range(chunks):
+        depth = depth_of(c)
+        host = chips - 1 - depth
+
+        def drain(j, carry):
+            @pl.when(z < host)
+            def _():
+                to_next(c, j).wait_send()
+
+            to_mate(c, j).wait_send()
+            return carry
+
+        @pl.when(z <= host)
+        def _():
+            lax.fori_loop(0, z + 1, drain, 0)
+
+        if depth:
+
+            @pl.when(z == host)
+            def _():
+                for d in range(1, depth + 1):
+                    to_mate(c, z + d).wait_send()
+                    give_back(c, d).wait_send()
+
+            @pl.when(z > host)
+            def _():
+                to_host(c).wait_send()
+                query_to_host(c, 1).wait_send()
 
 
 def shards(n_dp, n_seq, *args):
@@ -305,13 +393,14 @@
         out_specs=(vmem_spec, vmem_spec),
         scratch_shapes=[
             pltpu.VMEM((chunks, chips, 2, 2, rows, wide), BF16),
-            pltpu.VMEM((rows, width), BF16),
+            pltpu.VMEM((chunks, 3, 2, rows, wide), BF16),
+            pltpu.VMEM((chunks, 3, rows, wide + total_rank), BF16),
+            pltpu.VMEM((chunks, rows, wide + total_rank), BF16),
             pltpu.VMEM((rows, width), BF16),
             pltpu.VMEM((rows, model), BF16),
             pltpu.VMEM((model, total_rank), BF16),
             pltpu.VMEM((total_rank, width), BF16),
             pltpu.VMEM((experts, model), BF16),
-            pltpu.VMEM((rows, total_rank), BF16),
             pltpu.VMEM((rows, total_rank), BF16),
             pltpu.VMEM((rows, total_rank), F32),
             pltpu.VMEM((rows, experts), F32),
@@ -319,13 +408,16 @@
             pltpu.VMEM((n_seq, experts, piece), F32),
             pltpu.VMEM((n_dp, experts, piece), F32),
             pltpu.VMEM((n_seq, experts, piece), F32),
-            pltpu.VMEM((experts, piece), F32),
             dma((chunks, 2)),
-            dma((6,)),
+            dma((5 + chunks,)),
             dma((chunks, chips)),
             dma((chunks, chips)),
             dma((chunks, chips)),
             dma((chunks, chips)),
+            dma((chunks,)),
+            dma((chunks, 3)),
+            dma((chunks, 3)),
+            dma((chunks,)),
             dma((n_seq,)),
             dma((n_seq,)),
             dma((n_dp,)),

time: 121 us -> 118 us (0.975)
  Pallas kernels: 118 us -> 115 us
    pallas_call x1, Pallas kernels: 118 us -> 115 us  [shards(): pl.pallas_call(functools.partial(kernel, chips, chunks, heads, n_dp), out...]
where the time goes in v1:
time: 118 us
  Pallas kernels  115 us (97%)
  local copies, waits for them, and re-layouts  2.67 us (2%)
    pallas_call x1, Pallas kernels, shards(): pl.pallas_call(functools.partial(kernel, chips, chunks, heads, n_dp), out...  115 us
    unnamed x4, local copies, waits for them, and re-layouts  2.67 us

profile of v1, /device:TPU:0, one launch (start us, length us, event | category | flops | bytes accessed | tf_op | source)
XLA Modules:
  0.0 118.1 jit_solution(7752483100485851008)
XLA Ops:
  0.6 114.7 %shard_map.95 = (bf16[1,128,2560]{2,1,0:T(8,128)(2,1)}, f32[8,5120]{1,0:T(8,128)}) custom-call(bf16[1,128,2560]{2,1,0:T(8,128)(2,1)} %k_hbm.1, bf16[1,128,2560]{2,1,0:T(8,128)(2,1)} %v_hbm.1, bf16[1,128,2560]{2,1,0:T(8,128)(2,1)} %bq_hbm.1, bf16[1,128,2560]{2,1,0:T(8,128)(2,1)} %cot_hbm.1, bf16[1,128,5120]{2,1,0:T(8,128)(2,1)} %tok_hbm.1, ...), custom_call_target="tpu_custom_call" | custom-call | flops 3355443200 | bytes 5242880 | tf_op jit(solution)/shard_map/pallas_call | solution.py:386
  115.4 0.0 copy-start
  115.4 2.0 %copy.12 = bf16[1,128,2560]{2,1,0:T(8,128)(2,1)} copy(bf16[1,128,2560]{2,1,0:T(8,128)(2,1)} %get-tuple-element.4) | data formatting | bytes 1310720
  117.4 0.0 copy-done
  117.4 0.7 copy.13
Async XLA Ops:
  115.4 2.0 %copy-start = (f32[8,5120]{1,0:T(8,128)S(1)}, f32[8,5120]{1,0:T(8,128)}, u32[]{:S(2)}) copy-start(f32[8,5120]{1,0:T(8,128)} %get-tuple-element.5) | copy-start | bytes 491524

commit v2 on v1

--- a/solution.py
+++ b/solution.py
@@ -25,7 +25,7 @@
     chips, chunks, heads, n_dp,
     k_hbm, v_hbm, bq_hbm, cot_hbm, tok_hbm, down_hbm, up_hbm, gw_hbm,
     out_ref, gg_ref,
-    kv, qb, ob, back, bq, tok, down, up, gw, low, dmix, gates_ref, part, ra, rb, rc,
+    kv, qb, ob, back, sc, peak, bq, tok, down, up, gw, low, dmix, gates_ref, part, ra, rb, rc,
     own_sem, load_sem, up_send, up_recv, mate_send, mate_recv,
     q_send, q_recv, ret_send, ret_recv,
     a_send, a_recv, b_send, b_recv, c_send, c_recv,
@@ -171,41 +171,66 @@
         visible = lax.broadcasted_iota(jnp.int32, (rows, 2 * rows), 1) <= q_pos
         heads_at = [slice(h * HEAD_DIM, (h + 1) * HEAD_DIM) for h in range(heads)]
 
-        def block(j, states, masked):
+        def fold(x, op):
+            return op(x[:, :rows], x[:, rows:])
+
+        last = z + d
+
+        def score(j, h):
+            keys = kv[c, j, :, 0, :, heads_at[h]].reshape(2 * rows, HEAD_DIM)
+            return dot(qb[c, d, 0, :, heads_at[h]], keys, NT) * scale
+
+        tops = []
+        for h in range(heads):
+            found = jnp.where(visible, score(last, h), MASKED)
+            sc[h, last] = found
+            tops.append(fold(found, jnp.maximum))
+
+        def first_pass(j, tops):
+            new_tops = []
+            for h in range(heads):
+                found = score(j, h)
+                sc[h, j] = found
+                new_tops.append(jnp.maximum(tops[h], fold(found, jnp.maximum)))
+            return tuple(new_tops)
+
+        tops = lax.fori_loop(0, last, first_pass, tuple(tops))
+        for h in range(heads):
+            peak[h] = jnp.broadcast_to(
+                jnp.max(tops[h], axis=-1, keepdims=True), (rows, rows)
+            )
+
+        def second_pass(j, states):
             new_states = []
             for h in range(heads):
-                hcols = heads_at[h]
-                keys = kv[c, j, :, 0, :, hcols].reshape(2 * rows, HEAD_DIM)
-                values = kv[c, j, :, 1, :, hcols].reshape(2 * rows, HEAD_DIM)
-                scores = dot(qb[c, d, 0, :, hcols], keys, NT) * scale
-                slopes = dot(qb[c, d, 1, :, hcols], values, NT)
-                if masked:
-                    scores = jnp.where(visible, scores, MASKED)
-                top = jnp.max(scores, axis=-1, keepdims=True)
-                if states is not None:
-                    old_top, old_sum, old_delta, old_vk, old_grad = states[h]
-                    top = jnp.maximum(old_top, top)
-                weights = jnp.exp(scores - top)
+                total, delta, vk, grad = states[h]
+                keys = kv[c, j, :, 0, :, heads_at[h]].reshape(2 * rows, HEAD_DIM)
+                values = kv[c, j, :, 1, :, heads_at[h]].reshape(2 * rows, HEAD_DIM)
+                slopes = dot(qb[c, d, 1, :, heads_at[h]], values, NT)
+                top = peak[h]
+                weights = jnp.exp(sc[h, j] - jnp.concatenate([top, top], axis=1))
                 products = weights * slopes
-                total = jnp.sum(weights, axis=-1, keepdims=True)
-                delta = jnp.sum(products, axis=-1, keepdims=True)
-                vk = dot(weights.astype(BF16), jnp.concatenate([values, keys], axis=1))
-                grad = dot(products.astype(BF16), keys)
-                if states is not None:
-                    fade = jnp.exp(old_top - top)
-                    total = total + old_sum * fade
-                    delta = delta + old_delta * fade
-                    vk = vk + old_vk * fade
-                    grad = grad + old_grad * fade
-                new_states.append((top, total, delta, vk, grad))
+                new_states.append(
+                    (
+                        total + fold(weights, jnp.add),
+                        delta + fold(products, jnp.add),
+                        vk + dot(weights.astype(BF16), jnp.concatenate([values, keys], axis=1)),
+                        grad + dot(products.astype(BF16), keys),
+                    )
+                )
             return tuple(new_states)
 
-        states = block(z + d, None, True)
-        states = lax.fori_loop(0, z + d, lambda j, st: block(j, st, False), states)
+        empty = jnp.zeros((rows, rows), F32)
+        zero = jnp.zeros((rows, HEAD_DIM), F32)
+        zeros = jnp.zeros((rows, 2 * HEAD_DIM), F32)
+        states = lax.fori_loop(
+            0, last + 1, second_pass, ((empty, empty, zeros, zero),) * heads
+        )
         outs = []
         grads = []
-        for top, total, delta, vk, grad in states:
-            inverse = 1.0 / total
+        for total, delta, vk, grad in states:
+            inverse = 1.0 / jnp.sum(total, axis=-1, keepdims=True)
+            delta = jnp.sum(delta, axis=-1, keepdims=True)
             outs.append((vk[:, :HEAD_DIM] * inverse).astype(BF16))
             grads.append(
                 (
@@ -396,6 +421,8 @@
             pltpu.VMEM((chunks, 3, 2, rows, wide), BF16),
             pltpu.VMEM((chunks, 3, rows, wide + total_rank), BF16),
             pltpu.VMEM((chunks, rows, wide + total_rank), BF16),
+            pltpu.VMEM((heads, chips, rows, 2 * rows), F32),
+            pltpu.VMEM((heads, rows, rows), F32),
             pltpu.VMEM((rows, width), BF16),
             pltpu.VMEM((rows, model), BF16),
             pltpu.VMEM((model, total_rank), BF16),

time: 118 us -> 115 us (0.975)
  Pallas kernels: 115 us -> 111 us
    pallas_call x1, Pallas kernels: 115 us -> 111 us  [shards(): pl.pallas_call(functools.partial(kernel, chips, chunks, heads, n_dp), out...]
where the time goes in v2:
time: 115 us
  Pallas kernels  111 us (97%)
  local copies, waits for them, and re-layouts  2.67 us (2%)
    pallas_call x1, Pallas kernels, shards(): pl.pallas_call(functools.partial(kernel, chips, chunks, heads, n_dp), out...  111 us
    unnamed x4, local copies, waits for them, and re-layouts  2.67 us

profile of v2, /device:TPU:0, one launch (start us, length us, event | category | flops | bytes accessed | tf_op | source)
XLA Modules:
  0.0 114.7 jit_solution(6283671669763573681)
XLA Ops:
  0.6 111.4 %shard_map.95 = (bf16[1,128,2560]{2,1,0:T(8,128)(2,1)}, f32[8,5120]{1,0:T(8,128)}) custom-call(bf16[1,128,2560]{2,1,0:T(8,128)(2,1)} %k_hbm.1, bf16[1,128,2560]{2,1,0:T(8,128)(2,1)} %v_hbm.1, bf16[1,128,2560]{2,1,0:T(8,128)(2,1)} %bq_hbm.1, bf16[1,128,2560]{2,1,0:T(8,128)(2,1)} %cot_hbm.1, bf16[1,128,5120]{2,1,0:T(8,128)(2,1)} %tok_hbm.1, ...), custom_call_target="tpu_custom_call" | custom-call | flops 3355443200 | bytes 5242880 | tf_op jit(solution)/shard_map/pallas_call | solution.py:411
  112.0 0.0 copy-start
  112.1 2.0 %copy.12 = bf16[1,128,2560]{2,1,0:T(8,128)(2,1)} copy(bf16[1,128,2560]{2,1,0:T(8,128)(2,1)} %get-tuple-element.4) | data formatting | bytes 1310720
  114.1 0.0 copy-done
  114.1 0.7 copy.13
Async XLA Ops:
  112.0 2.0 %copy-start = (f32[8,5120]{1,0:T(8,128)S(1)}, f32[8,5120]{1,0:T(8,128)}, u32[]{:S(2)}) copy-start(f32[8,5120]{1,0:T(8,128)} %get-tuple-element.5) | copy-start | bytes 491524

commit v3 on v2

--- a/solution.py
+++ b/solution.py
@@ -51,7 +51,7 @@
         )
 
     def depth_of(c):
-        return min(max(0, 2 - (c + 1) // 2), chips - 1)
+        return min(1 if c < chunks // 2 else 0, chips - 1)
 
     def own_copies(c):
         cols = pl.ds(c * wide, wide)

time: 115 us -> 128 us (1.11)
  Pallas kernels: 111 us -> 125 us
    pallas_call x1, Pallas kernels: 111 us -> 125 us  [shards(): pl.pallas_call(functools.partial(kernel, chips, chunks, heads, n_dp), out...]
where the time goes in v3:
time: 128 us
  Pallas kernels  125 us (98%)
  local copies, waits for them, and re-layouts  2.67 us (2%)
    pallas_call x1, Pallas kernels, shards(): pl.pallas_call(functools.partial(kernel, chips, chunks, heads, n_dp), out...  125 us
    unnamed x4, local copies, waits for them, and re-layouts  2.67 us

profile of v3, /device:TPU:0, one launch (start us, length us, event | category | flops | bytes accessed | tf_op | source)
XLA Modules:
  0.0 127.9 jit_solution(2937174475889816660)
XLA Ops:
  0.6 124.6 %shard_map.95 = (bf16[1,128,2560]{2,1,0:T(8,128)(2,1)}, f32[8,5120]{1,0:T(8,128)}) custom-call(bf16[1,128,2560]{2,1,0:T(8,128)(2,1)} %k_hbm.1, bf16[1,128,2560]{2,1,0:T(8,128)(2,1)} %v_hbm.1, bf16[1,128,2560]{2,1,0:T(8,128)(2,1)} %bq_hbm.1, bf16[1,128,2560]{2,1,0:T(8,128)(2,1)} %cot_hbm.1, bf16[1,128,5120]{2,1,0:T(8,128)(2,1)} %tok_hbm.1, ...), custom_call_target="tpu_custom_call" | custom-call | flops 3355443200 | bytes 5242880 | tf_op jit(solution)/shard_map/pallas_call | solution.py:411
  125.2 0.0 copy-start
  125.2 2.0 %copy.12 = bf16[1,128,2560]{2,1,0:T(8,128)(2,1)} copy(bf16[1,128,2560]{2,1,0:T(8,128)(2,1)} %get-tuple-element.4) | data formatting | bytes 1310720
  127.2 0.0 copy-done
  127.2 0.7 copy.13
Async XLA Ops:
  125.2 2.0 %copy-start = (f32[8,5120]{1,0:T(8,128)S(1)}, f32[8,5120]{1,0:T(8,128)}, u32[]{:S(2)}) copy-start(f32[8,5120]{1,0:T(8,128)} %get-tuple-element.5) | copy-start | bytes 491524

commit v4 on v3

--- a/solution.py
+++ b/solution.py
@@ -51,7 +51,7 @@
         )
 
     def depth_of(c):
-        return min(1 if c < chunks // 2 else 0, chips - 1)
+        return min(max(0, 2 - c), chips - 1)
 
     def own_copies(c):
         cols = pl.ds(c * wide, wide)

time: 128 us -> 111 us (0.87)
  Pallas kernels: 125 us -> 107 us
    pallas_call x1, Pallas kernels: 125 us -> 107 us  [shards(): pl.pallas_call(functools.partial(kernel, chips, chunks, heads, n_dp), out...]
where the time goes in v4:
time: 111 us
  Pallas kernels  107 us (96%)
  local copies, waits for them, and re-layouts  2.67 us (2%)
    pallas_call x1, Pallas kernels, shards(): pl.pallas_call(functools.partial(kernel, chips, chunks, heads, n_dp), out...  107 us
    unnamed x4, local copies, waits for them, and re-layouts  2.67 us

profile of v4, /device:TPU:0, one launch (start us, length us, event | category | flops | bytes accessed | tf_op | source)
XLA Modules:
  0.0 110.5 jit_solution(8775745689987090633)
XLA Ops:
  0.6 107.2 %shard_map.95 = (bf16[1,128,2560]{2,1,0:T(8,128)(2,1)}, f32[8,5120]{1,0:T(8,128)}) custom-call(bf16[1,128,2560]{2,1,0:T(8,128)(2,1)} %k_hbm.1, bf16[1,128,2560]{2,1,0:T(8,128)(2,1)} %v_hbm.1, bf16[1,128,2560]{2,1,0:T(8,128)(2,1)} %bq_hbm.1, bf16[1,128,2560]{2,1,0:T(8,128)(2,1)} %cot_hbm.1, bf16[1,128,5120]{2,1,0:T(8,128)(2,1)} %tok_hbm.1, ...), custom_call_target="tpu_custom_call" | custom-call | flops 3355443200 | bytes 5242880 | tf_op jit(solution)/shard_map/pallas_call | solution.py:411
  107.9 0.0 copy-start
  107.9 2.0 %copy.12 = bf16[1,128,2560]{2,1,0:T(8,128)(2,1)} copy(bf16[1,128,2560]{2,1,0:T(8,128)(2,1)} %get-tuple-element.4) | data formatting | bytes 1310720
  109.9 0.0 copy-done
  109.9 0.7 copy.13
Async XLA Ops:
  107.9 2.0 %copy-start = (f32[8,5120]{1,0:T(8,128)S(1)}, f32[8,5120]{1,0:T(8,128)}, u32[]{:S(2)}) copy-start(f32[8,5120]{1,0:T(8,128)} %get-tuple-element.5) | copy-start | bytes 491524
